TPU v7x, 512 devices: a whole 4x4x16 slice. The times are simulated.
512 devices in a mesh: replica: 4 (over x), fsdp: 16 (over z_lo, y), tensor: 8 (over z_hi, core).
Axes of the slice: x: 4, y: 4, z: 16 (z_hi: 4, z_lo: 4; z = z_hi * 4 + z_lo), core: 2. Of those that a mesh axis runs over, the one named last changes fastest.
Arguments:
- tokens: bfloat16 [4, 4096, 8192], P('replica', 'fsdp', 'tensor'), may hold values from -6 to 6
- queries: bfloat16 [4, 4096, 8192], P('replica', 'fsdp', 'tensor'), may hold values from -68 to 68
- out_grad: bfloat16 [4, 4096, 8192], P('replica', 'fsdp', 'tensor'), may hold values from -6 to 6
- kv_weight: bfloat16 [4, 2, 8192, 1024], P('replica', None, 'fsdp', 'tensor'), may hold values from -0.0625 to 0.0625
- first_moment: bfloat16 [4, 2, 8192, 1024], P('replica', None, 'fsdp', 'tensor'), may hold values from -30 to 30
- second_moment: bfloat16 [4, 2, 8192, 1024], P('replica', None, 'fsdp', 'tensor'), may hold values from 20 to 2000
- pseudo_grads: float32 [4, 8192, 1024], P('replica', 'fsdp', 'tensor'), may hold values from -6 to 6
- outer_momentum: float32 [8192, 1024], P('fsdp', 'tensor'), may hold values from -6 to 6
- anchor: float32 [8192, 1024], P('fsdp', 'tensor'), may hold values from -6 to 6
Outputs:
- new_weight: bfloat16 [4, 2, 8192, 1024], P('replica', None, 'fsdp', 'tensor')
- new_first: bfloat16 [4, 2, 8192, 1024], P('replica', None, 'fsdp', 'tensor')
- new_second: bfloat16 [4, 2, 8192, 1024], P('replica', None, 'fsdp', 'tensor')
- new_anchor: float32 [8192, 1024], P('fsdp', 'tensor')
- new_momentum: float32 [8192, 1024], P('fsdp', 'tensor')
All inputs are finite; a program needn't handle non-finite values.
Results may differ from a plain program's by a relative error of at most 0.04.
Values may be sent and summed in bfloat16 or wider, within the bound.
A program may use at most 64 MiB of HBM per device.

v0:
```python
import jax
import jax.numpy as jnp
from jax import lax
from jax.sharding import PartitionSpec as P

HD = 128
STEP = 5


first_decay = 0.9
second_decay = 0.95
inner_rate = 0.001
weight_decay = 0.1
adam_epsilon = 1e-08
outer_rate = 0.7
outer_decay = 0.9


def attention_grads(query_rows, grad_rows, key_rows, value_rows):
    length = key_rows.shape[0]
    kv_heads = key_rows.shape[1] // HD
    members = query_rows.shape[1] // key_rows.shape[1]
    scaling = HD ** (-0.5)
    query_heads = query_rows.reshape(length, kv_heads, members, HD)
    grad_heads = grad_rows.reshape(length, kv_heads, members, HD)
    key_heads = key_rows.reshape(length, kv_heads, HD)
    value_heads = value_rows.reshape(length, kv_heads, HD)
    scores = (
        jnp.einsum("ihgd,jhd->hgij", query_heads, key_heads, preferred_element_type=jnp.float32)
        * scaling
    )
    causal = jnp.arange(length)[:, None] >= jnp.arange(length)[None, :]
    scores = jnp.where(causal, scores, -jnp.inf)
    probabilities = jax.nn.softmax(scores, axis=-1)
    rounded_probs = probabilities.astype(jnp.bfloat16)
    value_grads = jnp.einsum(
        "hgij,ihgd->jhd", rounded_probs, grad_heads, preferred_element_type=jnp.float32
    )
    prob_grads = jnp.einsum(
        "ihgd,jhd->hgij", grad_heads, value_heads, preferred_element_type=jnp.float32
    )
    row_delta = jnp.sum(probabilities * prob_grads, axis=-1, keepdims=True)
    score_grads = (probabilities * (prob_grads - row_delta) * scaling).astype(jnp.bfloat16)
    key_grads = jnp.einsum(
        "hgij,ihgd->jhd", score_grads, query_heads, preferred_element_type=jnp.float32
    )
    joined = jnp.concatenate(
        [key_grads.reshape(length, -1), value_grads.reshape(length, -1)], axis=1
    )
    return joined.astype(jnp.bfloat16)


def apply_adamw(weights, first_moment, second_moment, gradient):
    first_new = first_decay * first_moment.astype(jnp.float32) + (1.0 - first_decay) * gradient
    second_new = (
        second_decay * second_moment.astype(jnp.float32)
        + (1.0 - second_decay) * gradient * gradient
    )
    corrected_first = first_new / (1.0 - first_decay**STEP)
    corrected_second = second_new / (1.0 - second_decay**STEP)
    current = weights.astype(jnp.float32)
    updated = current - inner_rate * (
        corrected_first / (jnp.sqrt(corrected_second) + adam_epsilon) + weight_decay * current
    )
    return (
        updated.astype(jnp.bfloat16),
        first_new.astype(jnp.bfloat16),
        second_new.astype(jnp.bfloat16),
    )


def outer_step(averaged, momentum, anchor):
    momentum_new = outer_decay * momentum + averaged
    anchor_new = anchor - outer_rate * (averaged + outer_decay * momentum_new)
    return (anchor_new, momentum_new)


def shards(
    tokens,
    queries,
    out_grad,
    kv_weight,
    first_moment,
    second_moment,
    pseudo_grads,
    outer_momentum,
    anchor,
):
    token_rows = tokens[0]
    weights = kv_weight[0]
    gathered = lax.all_gather(token_rows, "tensor", axis=1, tiled=True)
    local_cols = weights.shape[2]
    weight_rows_here = weights.shape[1]
    columns = gathered
    projected = jnp.einsum(
        "td,kdc->ktc",
        columns,
        lax.all_gather(weights, "fsdp", axis=1, tiled=True),
        preferred_element_type=jnp.float32,
    )
    key_rows = projected[0].astype(jnp.bfloat16)
    value_rows = projected[1].astype(jnp.bfloat16)
    kv_grads = attention_grads(queries[0], out_grad[0], key_rows, value_rows)
    columns = gathered
    summed = lax.psum_scatter(
        lax.dot_general(
            columns, kv_grads, (((0,), (0,)), ((), ())), preferred_element_type=jnp.float32
        ).astype(jnp.bfloat16),
        "fsdp",
        scatter_dimension=0,
        tiled=True,
    ).astype(jnp.float32)
    gradient = summed.reshape(weight_rows_here, 2, local_cols).transpose(1, 0, 2)
    new_weight, new_first, new_second = apply_adamw(
        weights, first_moment[0], second_moment[0], gradient
    )
    own_term = pseudo_grads[0]
    replicas = lax.axis_size("replica")
    averaged = lax.psum(own_term.astype(jnp.bfloat16), "replica").astype(jnp.float32) / replicas
    new_anchor, new_momentum = outer_step(averaged, outer_momentum, anchor)
    return (new_weight[None], new_first[None], new_second[None], new_anchor, new_momentum)


def solution(mesh):
    return jax.shard_map(
        shards,
        mesh=mesh,
        in_specs=(
            P("replica", "fsdp", "tensor"),
            P("replica", "fsdp", "tensor"),
            P("replica", "fsdp", "tensor"),
            P("replica", None, "fsdp", "tensor"),
            P("replica", None, "fsdp", "tensor"),
            P("replica", None, "fsdp", "tensor"),
            P("replica", "fsdp", "tensor"),
            P("fsdp", "tensor"),
            P("fsdp", "tensor"),
        ),
        out_specs=(
            P("replica", None, "fsdp", "tensor"),
            P("replica", None, "fsdp", "tensor"),
            P("replica", None, "fsdp", "tensor"),
            P("fsdp", "tensor"),
            P("fsdp", "tensor"),
        ),
        check_vma=False,
    )
```

profile of v0, /device:TPU:6, one launch (start us, length us, event | category | flops | bytes accessed | tf_op | source)
XLA Modules:
  0.0 323.3 jit_solution(9365513488848936246)
XLA Ops:
  8.1 0.7 all-gather.7.cloned.1.call-update
  8.8 0.0 all-gather.5.cloned.1.call-start
  8.8 1.8 copy.14
  10.6 0.0 all-reduce.2.cloned.1.call-start
  10.7 1.6 convert_bitcast_fusion
  12.3 0.0 reduce-scatter.2.cloned.1.call-start
  12.4 0.1 copy.24
  12.5 0.1 copy.25
  12.6 99.6 %all-gather.7.cloned.1.call-done = bf16[1,256,8192]{2,1,0:T(8,128)(2,1)} async-done(((bf16[1,256,1024]{2,1,0:T(8,128)(2,1)}), bf16[1,256,8192]{2,1,0:T(8,128)(2,1)}) %all-gather.7.cloned.1.call-update) | async-done | bytes 4194320 | tf_op jit(solution)/shard_map/all_gather | solution.py:91
  112.2 90.9 %all-gather.5.cloned.1.call-done = bf16[1,2,8192,128]{2,3,1,0:T(8,128)(2,1)} async-done(((bf16[1,2,512,128]{2,3,1,0:T(8,128)(2,1)}), bf16[1,2,8192,128]{2,3,1,0:T(8,128)(2,1)}) %all-gather.5.cloned.1.call-update) | async-done | bytes 4194320 | tf_op jit(solution)/shard_map/all_gather | solution.py:98
  203.2 4.7 %fusion.16 = bf16[2,256,128]{1,2,0:T(8,128)(2,1)S(1)} fusion(bf16[1,256,8192]{2,1,0:T(8,128)(2,1)} %all-gather.7.cloned.1.call-done, bf16[1,2,8192,128]{2,3,1,0:T(8,128)(2,1)} %all-gather.5.cloned.1.call-done), kind=kOutput, calls=%fused_computation.17 | convolution fusion | flops 1073807360 | bytes 8519680 | tf_op jit(solution)/shard_map/td,kdc->ktc/dot_general | solution.py:95
  207.9 0.5 fusion.51
  208.4 0.3 fusion.10
  208.7 0.6 fusion.5
  209.3 0.6 fusion.22
  209.9 0.8 fusion.21
  210.7 1.4 copy-done
  212.1 3.2 fusion
  215.4 0.9 copy-done.4
  216.3 0.1 copy-done.5
  216.4 1.8 multiply_subtract_fusion
  218.1 95.4 %reduce-scatter.2.cloned.1.call-done = bf16[512,256]{0,1:T(8,128)(2,1)} async-done(((bf16[8192,256]{0,1:T(8,128)(2,1)}), bf16[512,256]{0,1:T(8,128)(2,1)}) %reduce-scatter.2.cloned.1.call-update) | async-done | bytes 262160 | tf_op jit(solution)/shard_map/reduce_scatter | solution.py:105
  313.5 1.1 copy.19
  314.6 1.5 fusion.41
  (19 shorter events, 0.2 us)
Async XLA Ops:
  8.0 4.4 %copy-start.2 = (bf16[1,256,1024]{2,1,0:T(8,128)(2,1)S(1)}, bf16[1,256,1024]{2,1,0:T(8,128)(2,1)}, u32[]{:S(2)}) copy-start(bf16[1,256,1024]{2,1,0:T(8,128)(2,1)} %param.10) | copy-start | bytes 1572868
  8.0 4.5 %copy-start.3 = (bf16[1,256,1024]{2,1,0:T(8,128)(2,1)S(1)}, bf16[1,256,1024]{2,1,0:T(8,128)(2,1)}, u32[]{:S(2)}) copy-start(bf16[1,256,1024]{2,1,0:T(8,128)(2,1)} %param.11) | copy-start | bytes 1572868
  8.0 104.2 %all-gather.7.cloned.1.call-start = ((), (), s32[]{:S(2)}) async-start(), calls=%async_computation.4 | async-start | bytes 4718592 | tf_op jit(solution)/shard_map/all_gather | solution.py:91
  8.8 194.4 %all-gather.5.cloned.1.call-start = ((), (), s32[]{:S(2)}) async-start(), calls=%async_computation.3 | async-start | bytes 4456448 | tf_op jit(solution)/shard_map/all_gather | solution.py:98
  10.6 204.8 %all-reduce.2.cloned.1.call-start = ((), (), s32[]{:S(2)}) async-start(), calls=%async_computation.2 | async-start | bytes 262144 | tf_op jit(solution)/shard_map/psum | solution.py:119
  12.3 301.2 %reduce-scatter.2.cloned.1.call-start = ((), (), s32[]{:S(2)}) async-start(), calls=%async_computation.1 | async-start | bytes 4456448 | tf_op jit(solution)/shard_map/reduce_scatter | solution.py:105
  209.9 2.2 copy-start
  215.3 0.9 copy-start.4
  215.3 1.0 copy-start.5
  215.3 99.3 %copy-start.1 = (bf16[1,2,512,128]{3,2,1,0:T(8,128)(2,1)S(1)}, bf16[1,2,512,128]{3,2,1,0:T(8,128)(2,1)}, u32[]{:S(2)}) copy-start(bf16[1,2,512,128]{3,2,1,0:T(8,128)(2,1)} %param.12) | copy-start | bytes 786436
  215.3 99.3 %copy-start.6 = (bf16[1,2,512,128]{3,2,1,0:T(8,128)(2,1)S(1)}, bf16[1,2,512,128]{3,2,1,0:T(8,128)(2,1)}, u32[]{:S(2)}) copy-start(bf16[1,2,512,128]{3,2,1,0:T(8,128)(2,1)} %param.14) | copy-start | bytes 786436
  215.3 99.3 %copy-start.7 = (bf16[1,2,512,128]{3,2,1,0:T(8,128)(2,1)S(1)}, bf16[1,2,512,128]{3,2,1,0:T(8,128)(2,1)}, u32[]{:S(2)}) copy-start(bf16[1,2,512,128]{3,2,1,0:T(8,128)(2,1)} %param.13) | copy-start | bytes 786436
Sparse Core Ops, SparseCore 0:
  11.0 101.1 all-gather.6
  114.9 88.2 all-gather.4
  215.5 97.9 reduce-scatter.1
Sparse Core Ops, SparseCore 1:
  14.0 59.7 all-reduce.1
where the time goes:
time: 324 us; the launch traced here: 323 us
  waiting for transfers between devices  287 us (89%)
  between operations  15.4 us (5%)
  matrix products  10.4 us (3%)
  local copies, waits for them, and re-layouts  5.41 us (2%)
  other arithmetic  5.23 us (2%)
    all_gather x1, waiting for transfers between devices, shards(): gathered = lax.all_gather(token_rows, 'tensor', axis=1, tiled=True)  99.6 us
    reduce_scatter x1, waiting for transfers between devices, shards(): lax.psum_scatter(lax.dot_general(columns, kv_grads, (((0,), (0,)), ((), (...  95.4 us
    all_gather x1, waiting for transfers between devices, shards(): lax.all_gather(weights, 'fsdp', axis=1, tiled=True)  90.9 us
  transfers between devices with their start and end apart: 4, of which 3 were waited for; matrix products, arithmetic and copies ran while one was open for 5% of the time, Pallas kernels for 0%

commit v1 on v0

--- a/solution.py
+++ b/solution.py
@@ -1,11 +1,15 @@
+import functools
+
 import jax
 import jax.numpy as jnp
 from jax import lax
+from jax.experimental import pallas as pl
+from jax.experimental.pallas import tpu as pltpu
 from jax.sharding import PartitionSpec as P
 
 HD = 128
 STEP = 5
-
+RING = 4
 
 first_decay = 0.9
 second_decay = 0.95
@@ -75,6 +79,269 @@
     return (anchor_new, momentum_new)
 
 
+def place():
+    f, t = lax.axis_index("fsdp"), lax.axis_index("tensor")
+    return f, t, f // RING, f % RING, t // 2, t % 2
+
+
+def at(z_low, y, z_high, core):
+    return {"fsdp": z_low * RING + y, "tensor": z_high * 2 + core}
+
+
+def send(src, dst, sems, slot, where):
+    return pltpu.make_async_remote_copy(
+        src_ref=src,
+        dst_ref=dst,
+        send_sem=sems[0].at[slot],
+        recv_sem=sems[1].at[slot],
+        device_id=where,
+        device_id_type=pl.DeviceIdType.MESH,
+    )
+
+
+def greet(partners):
+    barrier = pltpu.get_barrier_semaphore()
+    for partner in partners:
+        pl.semaphore_signal(
+            barrier, inc=1, device_id=partner, device_id_type=pl.DeviceIdType.MESH
+        )
+    pl.semaphore_wait(barrier, len(partners))
+
+
+def gather_kernel(
+    tok_ref, w_ref, tok_all, kv_ref, w_all, t_send, t_recv, l_send, l_recv, y_send, y_recv
+):
+    f, t, zl, y, zh, c = place()
+    up, down = at(zl, y, (zh + 1) % RING, c), at(zl, y, (zh + 3) % RING, c)
+    sibling = at(zl, y, zh, 1 - c)
+    right, left = at(zl, (y + 1) % RING, zh, c), at(zl, (y + 3) % RING, zh, c)
+    line = [at((zl + k) % RING, y, zh, c) for k in range(1, RING)]
+    greet([up, down, sibling, right, left] + line)
+
+    rows = tok_ref.shape[0]
+    half = rows // 2
+    top, bottom = pl.ds(0, half), pl.ds(half, half)
+    t_below = (zh + 3) % RING * 2 + c
+    t_above = (zh + 1) % RING * 2 + c
+    t_far = (zh + 2) % RING * 2 + c
+    flip = 1 - 2 * c
+    ts, ls, ys = (t_send, t_recv), (l_send, l_recv), (y_send, y_recv)
+    started = []
+
+    def go(copy):
+        copy.start()
+        started.append(copy)
+
+    for k in range(1, RING):
+        go(send(w_ref, w_all.at[f], ls, k - 1, line[k - 1]))
+    go(send(w_ref, w_all.at[f], ys, 0, right))
+    go(send(w_ref, w_all.at[f], ys, 1, left))
+    go(send(tok_ref, tok_all.at[t], ts, 0, up))
+    go(send(tok_ref, tok_all.at[t], ts, 1, down))
+    go(send(tok_ref, tok_all.at[t], ts, 2, sibling))
+    tok_all[t] = tok_ref[...]
+    w_all[f] = w_ref[...]
+
+    def arrived(ref, sems, slot):
+        send(ref, ref, sems, slot, sibling).wait_recv()
+
+    def pass_on(k):
+        z_from = (zl + RING - k) % RING
+        from_left = z_from * RING + (y + 3) % RING
+        from_right = z_from * RING + (y + 1) % RING
+        arrived(w_all.at[from_left], ys, 4 * k)
+        go(send(w_all.at[from_left, 0], w_all.at[from_left, 0], ys, 4 * k + 2, right))
+        arrived(w_all.at[from_right], ys, 4 * k + 1)
+        go(send(w_all.at[from_right, 1], w_all.at[from_right, 1], ys, 4 * k + 3, left))
+
+    for k in range(1, RING):
+        mine = (zl + RING - k) % RING * RING + y
+        arrived(w_all.at[mine], ls, k - 1)
+        go(send(w_all.at[mine], w_all.at[mine], ys, 4 * k, right))
+        go(send(w_all.at[mine], w_all.at[mine], ys, 4 * k + 1, left))
+        pass_on(k - 1)
+
+    arrived(tok_all.at[t_below], ts, 0)
+    go(send(tok_all.at[t_below, top], tok_all.at[t_below, top], ts, 3, up))
+    go(send(tok_all.at[t_below], tok_all.at[t_below], ts, 5, sibling))
+    arrived(tok_all.at[t_above], ts, 1)
+    go(send(tok_all.at[t_above, bottom], tok_all.at[t_above, bottom], ts, 4, down))
+    go(send(tok_all.at[t_above], tok_all.at[t_above], ts, 6, sibling))
+    pass_on(RING - 1)
+    for k in range(RING):
+        opposite = (zl + RING - k) % RING * RING + (y + 2) % RING
+        arrived(w_all.at[opposite, 0], ys, 4 * k + 2)
+        arrived(w_all.at[opposite, 1], ys, 4 * k + 3)
+
+    def term(block):
+        pair = w_all[pl.ds(2 * block, 2)]
+        piece = tok_all[block]
+        return [
+            jnp.dot(
+                piece,
+                pair[:, i].reshape(-1, pair.shape[-1]),
+                preferred_element_type=jnp.float32,
+            )
+            for i in range(2)
+        ]
+
+    def plus(a, b):
+        return [p + q for p, q in zip(a, b)]
+
+    total = term(t)
+    total = plus(total, term(t_below))
+    total = plus(total, term(t_above))
+    arrived(tok_all.at[t + flip], ts, 2)
+    total = plus(total, term(t + flip))
+    arrived(tok_all.at[t_below + flip], ts, 5)
+    total = plus(total, term(t_below + flip))
+    arrived(tok_all.at[t_above + flip], ts, 6)
+    total = plus(total, term(t_above + flip))
+    arrived(tok_all.at[t_far, top], ts, 3)
+    go(send(tok_all.at[t_far, top], tok_all.at[t_far, top], ts, 7, sibling))
+    arrived(tok_all.at[t_far, bottom], ts, 4)
+    go(send(tok_all.at[t_far, bottom], tok_all.at[t_far, bottom], ts, 8, sibling))
+    total = plus(total, term(t_far))
+    arrived(tok_all.at[t_far + flip, top], ts, 7)
+    arrived(tok_all.at[t_far + flip, bottom], ts, 8)
+    total = plus(total, term(t_far + flip))
+    kv_ref[0] = total[0].astype(kv_ref.dtype)
+    kv_ref[1] = total[1].astype(kv_ref.dtype)
+    for copy in started:
+        copy.wait_send()
+
+
+def scatter_kernel(
+    tok_all, grad_ref, out_ref, term, first, second, done, landed,
+    f_send, f_recv, s_send, s_recv, l_send, l_recv,
+):
+    f, t, zl, y, zh, c = place()
+    right, left = at(zl, (y + 1) % RING, zh, c), at(zl, (y + 3) % RING, zh, c)
+    line = [at((zl + k) % RING, y, zh, c) for k in range(1, RING)]
+    greet([right, left] + line)
+
+    fs, ss, ls = (f_send, f_recv), (s_send, s_recv), (l_send, l_recv)
+    width = out_ref.shape[1]
+    half = out_ref.shape[0] // 2
+    top, bottom = pl.ds(0, half), pl.ds(half, half)
+    grads = grad_ref[...]
+    started = []
+
+    def go(copy):
+        copy.start()
+        started.append(copy)
+
+    def make(z_to, y_to, slot):
+        block = z_to * RING + y_to
+        piece = tok_all[block // 2, :, pl.ds(pl.multiple_of(block % 2 * width, width), width)]
+        term[slot] = jnp.dot(grads, piece, preferred_element_type=jnp.float32).astype(term.dtype)
+
+    order = [1, 2, 3, 0]
+    for n, k in enumerate(order):
+        make((zl + k) % RING, (y + 2) % RING, 4 * n + 2)
+        go(send(term.at[4 * n + 2, top], first.at[n, top], fs, 2 * n, right))
+        go(send(term.at[4 * n + 2, bottom], first.at[n, bottom], fs, 2 * n + 1, left))
+    for n, k in enumerate(order):
+        z_to = (zl + k) % RING
+        make(z_to, (y + 1) % RING, 4 * n + 1)
+        make(z_to, (y + 3) % RING, 4 * n + 3)
+        make(z_to, y, 4 * n)
+
+    def arrived(ref, sems, slot):
+        send(ref, ref, sems, slot, right).wait_recv()
+
+    def add(slot, part, other):
+        term[slot, part] = (
+            term[slot, part].astype(jnp.float32) + other.astype(jnp.float32)
+        ).astype(term.dtype)
+
+    def middle(n):
+        arrived(first.at[n, top], fs, 2 * n)
+        add(4 * n + 1, top, first[n, top])
+        go(send(term.at[4 * n + 1], second.at[n, 0], ss, 2 * n, right))
+        arrived(first.at[n, bottom], fs, 2 * n + 1)
+        add(4 * n + 3, bottom, first[n, bottom])
+        go(send(term.at[4 * n + 3], second.at[n, 1], ss, 2 * n + 1, left))
+
+    def finish(n):
+        arrived(second.at[n, 0], ss, 2 * n)
+        arrived(second.at[n, 1], ss, 2 * n + 1)
+        total = (
+            term[4 * n].astype(jnp.float32)
+            + second[n, 0].astype(jnp.float32)
+            + second[n, 1].astype(jnp.float32)
+        )
+        k = order[n]
+        if k:
+            done[n] = total.astype(done.dtype)
+            go(send(done.at[n], landed.at[n], ls, n, line[k - 1]))
+        else:
+            out_ref[...] = total
+
+    middle(0)
+    for n in range(RING):
+        if n + 1 < RING:
+            middle(n + 1)
+        finish(n)
+    for n in range(RING - 1):
+        arrived(landed.at[n], ls, n)
+        out_ref[...] += landed[n].astype(jnp.float32)
+    for copy in started:
+        copy.wait_send()
+
+
+def gather(tokens, weights):
+    rows, depth = tokens.shape
+    vmem = pl.BlockSpec(memory_space=pltpu.VMEM)
+    sems = pltpu.SemaphoreType.DMA
+    return pl.pallas_call(
+        gather_kernel,
+        out_shape=(
+            jax.ShapeDtypeStruct((8, rows, depth), jnp.bfloat16),
+            jax.ShapeDtypeStruct((2, rows, HD), jnp.bfloat16),
+        ),
+        in_specs=[vmem] * 2,
+        out_specs=(vmem, vmem),
+        scratch_shapes=[
+            pltpu.VMEM((16,) + weights.shape, jnp.bfloat16),
+            sems((9,)), sems((9,)),
+            sems((3,)), sems((3,)),
+            sems((16,)), sems((16,)),
+        ],
+        compiler_params=pltpu.CompilerParams(
+            collective_id=0, has_side_effects=True, vmem_limit_bytes=48 * 2**20
+        ),
+        name="gather_project",
+    )(tokens, weights)
+
+
+def scatter(tok_all, grads_t, width):
+    features = grads_t.shape[0]
+    vmem = pl.BlockSpec(memory_space=pltpu.VMEM)
+    sems = pltpu.SemaphoreType.DMA
+    block = (features, width)
+    return pl.pallas_call(
+        scatter_kernel,
+        out_shape=jax.ShapeDtypeStruct(block, jnp.float32),
+        in_specs=[vmem] * 2,
+        out_specs=vmem,
+        scratch_shapes=[
+            pltpu.VMEM((16,) + block, jnp.bfloat16),
+            pltpu.VMEM((4,) + block, jnp.bfloat16),
+            pltpu.VMEM((4, 2) + block, jnp.bfloat16),
+            pltpu.VMEM((3,) + block, jnp.bfloat16),
+            pltpu.VMEM((3,) + block, jnp.bfloat16),
+            sems((8,)), sems((8,)),
+            sems((8,)), sems((8,)),
+            sems((3,)), sems((3,)),
+        ],
+        compiler_params=pltpu.CompilerParams(
+            collective_id=1, has_side_effects=True, vmem_limit_bytes=48 * 2**20
+        ),
+        name="gradient_scatter",
+    )(tok_all, grads_t)
+
+
 def shards(
     tokens,
     queries,
@@ -86,38 +353,19 @@
     outer_momentum,
     anchor,
 ):
-    token_rows = tokens[0]
     weights = kv_weight[0]
-    gathered = lax.all_gather(token_rows, "tensor", axis=1, tiled=True)
-    local_cols = weights.shape[2]
-    weight_rows_here = weights.shape[1]
-    columns = gathered
-    projected = jnp.einsum(
-        "td,kdc->ktc",
-        columns,
-        lax.all_gather(weights, "fsdp", axis=1, tiled=True),
-        preferred_element_type=jnp.float32,
-    )
-    key_rows = projected[0].astype(jnp.bfloat16)
-    value_rows = projected[1].astype(jnp.bfloat16)
-    kv_grads = attention_grads(queries[0], out_grad[0], key_rows, value_rows)
-    columns = gathered
-    summed = lax.psum_scatter(
-        lax.dot_general(
-            columns, kv_grads, (((0,), (0,)), ((), ())), preferred_element_type=jnp.float32
-        ).astype(jnp.bfloat16),
-        "fsdp",
-        scatter_dimension=0,
-        tiled=True,
-    ).astype(jnp.float32)
-    gradient = summed.reshape(weight_rows_here, 2, local_cols).transpose(1, 0, 2)
-    new_weight, new_first, new_second = apply_adamw(
-        weights, first_moment[0], second_moment[0], gradient
-    )
     own_term = pseudo_grads[0]
     replicas = lax.axis_size("replica")
     averaged = lax.psum(own_term.astype(jnp.bfloat16), "replica").astype(jnp.float32) / replicas
     new_anchor, new_momentum = outer_step(averaged, outer_momentum, anchor)
+
+    tok_all, kv = gather(tokens[0], weights)
+    kv_grads = attention_grads(queries[0], out_grad[0], kv[0], kv[1])
+    summed = scatter(tok_all, kv_grads.T, weights.shape[1])
+    gradient = summed.reshape(2, HD, weights.shape[1]).transpose(0, 2, 1)
+    new_weight, new_first, new_second = apply_adamw(
+        weights, first_moment[0], second_moment[0], gradient
+    )
     return (new_weight[None], new_first[None], new_second[None], new_anchor, new_momentum)
 
 

time: 324 us -> 182 us (0.56)
  waiting for transfers between devices: 287 us -> 0.02 us
  Pallas kernels: 0 us -> 157 us
  matrix products: 10.4 us -> 2.2 us
    all_gather x2 -> x0, waiting for transfers between devices: 191 us -> none  [the longest x1 99.6 us: shards(): gathered = lax.all_gather(token_rows, 'tensor', axis=1, tiled=True)]
    pallas_call x0 -> x2, Pallas kernels: none -> 157 us  [the longest x1 90 us: gather(): pl.pallas_call(gather_kernel, out_shape=(jax.ShapeDtypeStruct((8, rows, d...]
    reduce_scatter x1 -> x0, waiting for transfers between devices: 95.4 us -> none  [shards(): lax.psum_scatter(lax.dot_general(columns, kv_grads, (((0,), (0,)), ((), (...]
    dot_general x2 -> x0, matrix products: 7.97 us -> none  [the longest x1 4.74 us: shards(): jnp.einsum('td,kdc->ktc', columns, lax.all_gather(weights, 'fsdp', axis=1...]
    unnamed x19 -> x12, local copies, waits for them, and re-layouts: 4.33 us -> 0.03 us
  transfers between devices with their start and end apart: 4 -> 1, of which waited for: 3 -> 0; matrix products, arithmetic and copies ran while one was open for 5% -> 4% of each run, Pallas kernels for 0% -> 87%
where the time goes in v1:
time: 182 us; the launch traced here: 181 us
  Pallas kernels  157 us (86%)
  between operations  14.2 us (8%)
  other arithmetic  5.3 us (3%)
  local copies, waits for them, and re-layouts  2.71 us (1%)
  matrix products  2.2 us (1%)
    pallas_call x1, Pallas kernels, gather(): pl.pallas_call(gather_kernel, out_shape=(jax.ShapeDtypeStruct((8, rows, d...  90 us
    pallas_call x1, Pallas kernels, scatter(): pl.pallas_call(scatter_kernel, out_shape=jax.ShapeDtypeStruct(block, jnp....  67 us
  transfers between devices with their start and end apart: 1, of which 0 were waited for; matrix products, arithmetic and copies ran while one was open for 4% of the time, Pallas kernels for 87%

profile of v1, /device:TPU:6, one launch (start us, length us, event | category | flops | bytes accessed | tf_op | source)
XLA Modules:
  0.0 181.5 jit_solution(12922313792577073757)
XLA Ops:
  7.2 0.0 copy-start
  7.2 0.0 copy-start.1
  7.2 0.0 all-reduce.2.cloned.1.call-start
  7.2 1.7 convert_bitcast_fusion
  8.9 0.0 all-reduce.2.cloned.1.call-update
  9.0 1.2 copy.23
  10.2 1.2 copy.24
  11.5 0.0 copy-done
  11.5 0.0 copy-done.1
  11.5 90.0 %gather_project.1 = (bf16[8,256,1024]{2,1,0:T(8,128)(2,1)S(1)}, bf16[2,256,128]{2,1,0:T(8,128)(2,1)S(1)}) custom-call(bf16[256,1024]{1,0:T(8,128)(2,1)S(1)} %bitcast.107, bf16[2,512,128]{2,1,0:T(8,128)(2,1)S(1)} %bitcast.106), custom_call_target="tpu_custom_call" | custom-call | tf_op jit(solution)/shard_map/gather_project/pallas_call | solution.py:297
  101.5 0.4 fusion.32
  102.0 0.3 fusion.5
  102.3 0.5 fusion
  102.8 0.5 fusion.7
  103.3 0.7 fusion.6
  104.1 0.0 copy-start.4
  104.1 0.0 copy-start.5
  104.1 67.0 %gradient_scatter.1 = f32[256,512]{1,0:T(8,128)S(1)} custom-call(bf16[8,256,1024]{2,1,0:T(8,128)(2,1)S(1)} %get-tuple-element.7.tok_all, bf16[256,256]{1,0:T(8,128)(2,1)S(1)} %maximum_bitcast_fusion.grad_ref), custom_call_target="tpu_custom_call" | custom-call | tf_op jit(solution)/shard_map/gradient_scatter/pallas_call | solution.py:323
  171.1 0.0 copy-start.2
  171.1 0.0 copy-start.3
  171.1 0.2 copy.20
  171.3 0.0 copy-done.4
  171.4 1.5 fusion.21
  172.9 1.8 multiply_subtract_fusion
  (6 shorter events, 0.0 us)
Async XLA Ops:
  7.2 4.3 %copy-start = (bf16[1,2,512,128]{3,2,1,0:T(8,128)(2,1)S(1)}, bf16[1,2,512,128]{3,2,1,0:T(8,128)(2,1)}, u32[]{:S(2)}) copy-start(bf16[1,2,512,128]{3,2,1,0:T(8,128)(2,1)} %param.12) | copy-start | bytes 786436
  7.2 4.3 %copy-start.1 = (bf16[1,256,1024]{2,1,0:T(8,128)(2,1)S(1)}, bf16[1,256,1024]{2,1,0:T(8,128)(2,1)}, u32[]{:S(2)}) copy-start(bf16[1,256,1024]{2,1,0:T(8,128)(2,1)} %param.9) | copy-start | bytes 1572868
  7.2 165.7 %all-reduce.2.cloned.1.call-start = ((), (), s32[]{:S(2)}) async-start(), calls=%async_computation | async-start | bytes 262144 | tf_op jit(solution)/shard_map/psum | solution.py:359
  104.1 67.3 %copy-start.4 = (bf16[1,2,512,128]{3,2,1,0:T(8,128)(2,1)S(1)}, bf16[1,2,512,128]{3,2,1,0:T(8,128)(2,1)}, u32[]{:S(2)}) copy-start(bf16[1,2,512,128]{3,2,1,0:T(8,128)(2,1)} %param.14) | copy-start | bytes 786436
  104.1 67.3 %copy-start.5 = (bf16[1,2,512,128]{3,2,1,0:T(8,128)(2,1)S(1)}, bf16[1,2,512,128]{3,2,1,0:T(8,128)(2,1)}, u32[]{:S(2)}) copy-start(bf16[1,2,512,128]{3,2,1,0:T(8,128)(2,1)} %param.13) | copy-start | bytes 786436
  171.1 1.8 copy-start.2
  171.1 1.8 copy-start.3
Sparse Core Ops, SparseCore 0:
  10.9 59.8 all-reduce.1
